TPU v7x, 32 devices: a whole 2x2x4 slice. The times are simulated.
32 devices in a mesh: seq: 8 (over z, y), tp: 4 (over x, core).
Axes of the slice: x: 2, y: 2, z: 4, core: 2. Of those that a mesh axis runs over, the one named last changes fastest.
Arguments:
- q_new: bfloat16 [4096, 8192], P('seq', 'tp'), may hold values from -16 to 16
- k_new: bfloat16 [4096, 1024], P('seq', 'tp'), may hold values from -6 to 6
- v_new: bfloat16 [4096, 1024], P('seq', 'tp'), may hold values from -6 to 6
- q_bias: bfloat16 [8192], P('tp'), may hold values from -3 to 3
- k_bias: bfloat16 [1024], P('tp'), may hold values from -3 to 3
- v_bias: bfloat16 [1024], P('tp'), may hold values from -3 to 3
- cache_k: bfloat16 [16384, 1024], P('seq', 'tp'), may hold values from -16 to 16
- cache_v: bfloat16 [16384, 1024], P('seq', 'tp'), may hold values from -6 to 6
- deal: int32 [8], replicated, may hold values from 0 to 7, each once
- cache_len: int32 [8], replicated, may hold values from 1 to 2048, 8192 in all
Outputs:
- attn_out: bfloat16 [4096, 8192], P('seq', 'tp')
- new_keys: bfloat16 [4096, 1024], P('seq', 'tp')
- new_values: bfloat16 [4096, 1024], P('seq', 'tp')
- last_norm: float32 [8], P('seq')
- top_logit: float32 [8], P('seq')
Inputs may be any that keep to these rules, and one draw needn't show every extreme that they name: `deal`: each request fills exactly one slot. `cache_len`: the lengths sum to 8192 and the largest is exactly 2048.
All inputs are finite; a program needn't handle non-finite values.
Results may differ from a plain program's by a relative error of at most 0.012.
Values may be sent and summed in bfloat16 or wider, within the bound.
No kernel may reach another device: no remote copies, remote signals or barrier semaphores. Data moves between devices by JAX's collectives and lax.ppermute only.
A program may use at most 192 MiB of HBM per device.

v0:
```python
import functools
import math

import jax
import jax.numpy as jnp
from jax import lax
from jax.experimental import pallas as pl
from jax.experimental.pallas import tpu as pltpu
from jax.sharding import PartitionSpec as P

HEAD = 128
LOG2E = 1.4426950408889634
theta_base = 1000000.0
masked_score = -1e30
norm_epsilon = 1e-06
f32, bf16 = jnp.float32, jnp.bfloat16

SAFE = 60.0
ROWS_T = (((1,), (1,)), ((), ()))
PLAIN = (((1,), (0,)), ((), ()))
ANY = pl.BlockSpec(memory_space=pl.ANY)
SMEM = pl.BlockSpec(memory_space=pltpu.SMEM)


def fold(x):
    part = x[:, :HEAD]
    for j in range(1, x.shape[1] // HEAD):
        part = part + x[:, j * HEAD : (j + 1) * HEAD]
    return part


def twice(x):
    return jnp.concatenate([x, x], axis=1)


def attend_kernel(*refs, skip, offset, size, period, group, wide_block, block, tail):
    meta, arrived, q_bias, cos, sin, ck, cv, nk, nv, norms = refs[:10]
    o_ref, stat, qs, m_s, l_s, acc = refs[-6:]
    length = meta[0]
    scale = HEAD**-0.5 * LOG2E
    pieces = arrived.shape[0]
    rows = pieces * size
    for e in range(pieces):
        here = slice(e * period + offset, e * period + offset + size)
        c, s = cos[here, :], sin[here, :]
        for h in range(group):
            column = slice(h * HEAD, (h + 1) * HEAD)
            x = arrived[e, skip : skip + size, column].astype(f32) + q_bias[:, column].astype(f32)
            y = (x * c + pltpu.roll(x, HEAD // 2, 1) * s).astype(bf16).astype(f32)
            z = y * scale
            high = z.astype(bf16)
            at = slice(h * rows + e * size, h * rows + (e + 1) * size)
            qs[at, :HEAD] = high
            qs[at, HEAD:] = (z - high.astype(f32)).astype(bf16)
    high = qs[:, :HEAD].astype(f32)
    lengths = lax.dot_general(
        (high * high).astype(bf16), jnp.ones((HEAD, HEAD), bf16), PLAIN, preferred_element_type=f32
    )
    biggest = jnp.max(lengths.reshape(group * rows // 8, 8, HEAD), axis=0)
    bound = jnp.max(biggest) * jnp.max(norms[...])
    l_s[...] = jnp.zeros(l_s.shape, f32)
    acc[...] = jnp.zeros(acc.shape, f32)
    whole = length // wide_block
    rest = whole * (wide_block // block)
    cached = (length + block - 1) // block

    def causal(heads, width):
        shape = (heads * pieces, size, width)
        piece = lax.broadcasted_iota(jnp.int32, shape, 0) % pieces
        row = (piece * period + lax.broadcasted_iota(jnp.int32, shape, 1)).reshape(heads * rows, width)
        return lax.broadcasted_iota(jnp.int32, (heads * rows, width), 1) - row <= offset

    @pl.when(bound <= SAFE * SAFE)
    def _():
        def add(k, v, valid):
            weight = jnp.exp2(lax.dot_general(qs[...], twice(k), ROWS_T, preferred_element_type=f32))
            if valid is not None:
                weight = jnp.where(valid, weight, 0.0)
            l_s[...] += fold(weight)
            acc[...] += lax.dot_general(weight.astype(bf16), v, PLAIN, preferred_element_type=f32)

        def full(i, carry):
            at = pl.ds(pl.multiple_of(i * wide_block, wide_block), wide_block)
            add(ck[at, :], cv[at, :], None)
            return carry

        def partial(i, carry):
            at = pl.ds(pl.multiple_of(i * block, block), block)
            key = lax.broadcasted_iota(jnp.int32, (group * rows, block), 1)
            add(ck[at, :], cv[at, :], key < length - i * block)
            return carry

        lax.fori_loop(0, whole, full, 0)
        lax.fori_loop(rest, cached, partial, 0)
        add(nk[...], nv[...], causal(group, nk.shape[0]))

    @pl.when(bound > SAFE * SAFE)
    def _():
        m_s[...] = jnp.full(m_s.shape, masked_score, f32)

        def online(k, v, valid):
            def piece(h, carry):
                at = pl.ds(pl.multiple_of(h * rows, 16), rows)
                scores = lax.dot_general(qs[at, :], twice(k), ROWS_T, preferred_element_type=f32)
                scores = jnp.where(valid, scores, masked_score)
                old = m_s[at, :]
                new = jnp.maximum(old, jnp.max(scores, axis=1, keepdims=True))
                m_s[at, :] = new
                weight = jnp.exp2(scores - jnp.tile(new, (1, k.shape[0] // HEAD)))
                factor = jnp.exp2(old - new)
                l_s[at, :] = l_s[at, :] * factor + fold(weight)
                acc[at, :] = acc[at, :] * factor + lax.dot_general(
                    weight.astype(bf16), v, PLAIN, preferred_element_type=f32
                )
                return carry

            lax.fori_loop(0, group, piece, 0)

        def step(i, carry):
            at = pl.ds(pl.multiple_of(i * block, block), block)
            key = lax.broadcasted_iota(jnp.int32, (rows, block), 1)
            online(ck[at, :], cv[at, :], key < length - i * block)
            return carry

        lax.fori_loop(0, cached, step, 0)
        online(nk[...], nv[...], causal(1, nk.shape[0]))

    squares = jnp.zeros((8, HEAD), f32)
    for h in range(group):
        at = slice(h * rows, (h + 1) * rows)
        mixture = acc[at, :] / jnp.sum(l_s[at, :], axis=1, keepdims=True)
        o_ref[:, :, h * HEAD : (h + 1) * HEAD] = mixture.astype(bf16).reshape(pieces, size, HEAD)
        end = mixture[rows - 8 :, :]
        squares = squares + end * end
    if tail:
        last = jnp.concatenate([qs[(h + 1) * rows - 16 : (h + 1) * rows, :] for h in range(group)], axis=0)
        old_scores = lax.dot_general(twice(ck[...]), last, ROWS_T, preferred_element_type=f32)
        key = lax.broadcasted_iota(jnp.int32, old_scores.shape, 0)
        old_scores = jnp.where(key < length, old_scores, masked_score)
        new_scores = lax.dot_general(twice(nk[...]), last, ROWS_T, preferred_element_type=f32)
        top = jnp.maximum(
            jnp.max(old_scores.reshape(-1, 8, group * 16), axis=0),
            jnp.max(new_scores.reshape(-1, 8, group * 16), axis=0),
        )
        lane = lax.broadcasted_iota(jnp.int32, top.shape, 1)
        top = jnp.where(lane % 16 == 15, top, masked_score)
        stat[0:8, :] = squares
        stat[8:16, :] = jnp.max(top, axis=(0, 1), keepdims=True) * (1.0 / LOG2E) + jnp.zeros((8, HEAD), f32)
    else:
        stat[...] = jnp.zeros_like(stat)


def attend(meta, arrived, bias, angles, caches, news, norms, out, offset, size, tail, kv_heads):
    pieces, height, q_cols = arrived.shape
    rows = pieces * size
    group = q_cols // HEAD // kv_heads
    wide = group * HEAD
    fresh, cache_rows = news[0].shape[0], caches[0].shape[0]
    period = fresh // pieces
    wide_block, block = math.gcd(1024, cache_rows), math.gcd(512, cache_rows)
    column = lambda n, width: pl.BlockSpec((n, width), lambda g, m: (0, g))
    table = pl.BlockSpec((fresh, HEAD), lambda g, m: (0, 0))
    given = [] if out is None else [out]
    spec = pltpu.PrefetchScalarGridSpec(
        num_scalar_prefetch=1,
        grid=(kv_heads,),
        in_specs=[
            pl.BlockSpec((pieces, height, wide), lambda g, m: (0, 0, g)), column(1, wide), table, table,
            column(cache_rows, HEAD), column(cache_rows, HEAD), column(fresh, HEAD), column(fresh, HEAD), column(8, HEAD),
        ] + [ANY] * len(given),
        out_specs=[pl.BlockSpec((pieces, size, wide), lambda g, m: (0, offset // size, g)), column(16, HEAD)],
        scratch_shapes=[
            pltpu.VMEM((group * rows, 2 * HEAD), bf16),
            pltpu.VMEM((group * rows, HEAD), f32),
            pltpu.VMEM((group * rows, HEAD), f32),
            pltpu.VMEM((group * rows, HEAD), f32),
        ],
    )
    work = kv_heads * group * rows * (cache_rows // 2 + fresh)
    return pl.pallas_call(
        functools.partial(
            attend_kernel, skip=height - size, offset=offset, size=size, period=period, group=group,
            wide_block=wide_block, block=block, tail=tail,
        ),
        grid_spec=spec,
        out_shape=[
            jax.ShapeDtypeStruct((pieces, period, q_cols), bf16),
            jax.ShapeDtypeStruct((16, kv_heads * HEAD), f32),
        ],
        input_output_aliases={10: 0} if given else {},
        compiler_params=pltpu.CompilerParams(vmem_limit_bytes=60 << 20),
        cost_estimate=pl.CostEstimate(
            flops=4 * work * HEAD, bytes_accessed=4 * cache_rows * HEAD * kv_heads, transcendentals=work
        ),
        name="attend",
    )(meta, arrived, bias, *angles, *caches, *news, norms, *given)


def tables(length, rows):
    half = HEAD // 2
    frequency = theta_base ** (-2.0 * jnp.arange(half, dtype=f32) / HEAD)
    positions = length + jnp.arange(rows, dtype=jnp.int32)
    angles = positions.astype(f32)[:, None] * frequency[None, :]
    cosine, sine = jnp.cos(angles), jnp.sin(angles)
    return jnp.concatenate([cosine, cosine], 1), jnp.concatenate([-sine, sine], 1)


def longest(keys, valid):
    wide = keys.astype(f32)
    squares = (wide * wide).astype(bf16)
    sums = lax.dot_general(squares, jnp.ones((HEAD, HEAD), bf16), PLAIN, preferred_element_type=f32)
    if valid is not None:
        sums = jnp.where(lax.broadcasted_iota(jnp.int32, sums.shape, 0) < valid, sums, 0.0)
    return jnp.max(sums.reshape(sums.shape[0] // 8, 8, HEAD), axis=0) * 1.05


def fresh_kernel(meta, arrived, k_bias, v_bias, cos, sin, ck, k_out, v_out, norms, *, size, packs):
    length = meta[0]
    cols = k_out.shape[1]
    for e in range(arrived.shape[0]):
        for b in range(packs):
            here = slice((e * packs + b) * size, (e * packs + b + 1) * size)
            raw = arrived[e, :size, 2 * cols * b : 2 * cols * (b + 1)].astype(f32)
            c, s = cos[here, :], sin[here, :]
            for h in range(cols // HEAD):
                column = slice(h * HEAD, (h + 1) * HEAD)
                x = raw[:, column] + k_bias[:, column].astype(f32)
                k_out[here, column] = (x * c + pltpu.roll(x, HEAD // 2, 1) * s).astype(bf16)
            v_out[here, :] = (raw[:, cols:] + v_bias[...].astype(f32)).astype(bf16)
    for h in range(cols // HEAD):
        column = slice(h * HEAD, (h + 1) * HEAD)
        norms[:, column] = jnp.maximum(longest(k_out[:, column], None), longest(ck[:, column], length))


def fresh_rows(meta, arrived, k_bias, v_bias, angles, cache_k, size):
    pieces, _, width = arrived.shape
    cols = k_bias.shape[1]
    packs = width // (2 * cols)
    total = pieces * packs * size
    whole = pl.BlockSpec(memory_space=pltpu.VMEM)
    return pl.pallas_call(
        functools.partial(fresh_kernel, size=size, packs=packs),
        in_specs=[SMEM] + [whole] * 6,
        out_specs=[whole] * 3,
        out_shape=[
            jax.ShapeDtypeStruct((total, cols), bf16),
            jax.ShapeDtypeStruct((total, cols), bf16),
            jax.ShapeDtypeStruct((8, cols), f32),
        ],
        compiler_params=pltpu.CompilerParams(vmem_limit_bytes=32 << 20),
        name="fresh",
    )(meta, arrived, k_bias, v_bias, *angles, cache_k)


def swap_tp(pair, step):
    size = lax.axis_size("tp")
    return lax.ppermute(pair, "tp", [(i, i ^ step) for i in range(size)])


def run_copies(copies):
    for copy in copies:
        copy.start()
    for copy in copies:
        copy.wait()


def deal_kernel(q, k, v, out, held, sems, *, packs):
    pieces, height, _ = held.shape
    size = q.shape[0] // pieces
    kv_size = height - size
    copies = []
    for e in range(pieces):
        copies.append((q.at[pl.ds(e * size, size)], held.at[e, pl.ds(kv_size, size)]))
        for b in range(packs):
            rows = pl.ds((e * packs + b) * kv_size, kv_size)
            for n, x in enumerate((k, v)):
                width = x.shape[1]
                copies.append((x.at[rows], held.at[e, pl.ds(0, kv_size), pl.ds((2 * b + n) * width, width)]))
    run_copies([pltpu.make_async_copy(a, b, sems.at[n]) for n, (a, b) in enumerate(copies)])
    run_copies([pltpu.make_async_copy(held, out, sems.at[0])])


def deal_pieces(q, k, v, pieces, packs):
    total, q_cols = q.shape
    shape = (pieces, total // pieces + total // pieces // packs, q_cols)
    return pl.pallas_call(
        functools.partial(deal_kernel, packs=packs),
        in_specs=[ANY] * 3,
        out_specs=ANY,
        out_shape=jax.ShapeDtypeStruct(shape, bf16),
        scratch_shapes=[pltpu.VMEM(shape, bf16), pltpu.SemaphoreType.DMA((pieces * (1 + 2 * packs),))],
        compiler_params=pltpu.CompilerParams(vmem_limit_bytes=60 << 20),
        name="deal",
    )(q, k, v)


def route_kernel(deal, x, out, held, sems, *, spans):
    slots = x.shape[0]
    into, back = [], []
    for s in range(slots):
        base = 0
        for n, (offset, size) in enumerate(spans):
            into.append(pltpu.make_async_copy(x.at[s, pl.ds(offset, size)], held.at[s, pl.ds(base, size)], sems.at[n, s]))
            base += size
        back.append(pltpu.make_async_copy(held.at[s], out.at[deal[s]], sems.at[0, s]))
    run_copies(into)
    run_copies(back)


def route(deal, x, spans):
    slots, _, q_cols = x.shape
    shape = (slots, sum(size for _, size in spans), q_cols)
    return pl.pallas_call(
        functools.partial(route_kernel, spans=spans),
        in_specs=[SMEM, ANY],
        out_specs=ANY,
        out_shape=jax.ShapeDtypeStruct(shape, bf16),
        scratch_shapes=[pltpu.VMEM(shape, bf16), pltpu.SemaphoreType.DMA((len(spans), slots))],
        compiler_params=pltpu.CompilerParams(vmem_limit_bytes=60 << 20),
        name="route",
    )(deal, x)


def cut_rows(period):
    return [(period // 2, period // 2), (0, period // 2)]


def body(q_new, k_new, v_new, q_bias, k_bias, v_bias, cache_k, cache_v, deal, cache_len):
    slots = lax.axis_size("seq")
    own = lax.axis_index("seq").astype(jnp.int32)
    slot_ids = jnp.arange(slots, dtype=jnp.int32)
    length = jnp.sum(jnp.where(slot_ids == own, cache_len, 0))
    total, q_cols = q_new.shape
    kv_cols = k_new.shape[1]
    kv_heads = kv_cols // HEAD
    packs = q_cols // (2 * kv_cols)
    q_bias, k_bias, v_bias = (x.reshape(1, -1) for x in (q_bias, k_bias, v_bias))
    angles = tables(length, total)
    caches = (cache_k, cache_v)
    meta = jnp.stack([length, own])

    def exchange(x):
        return lax.all_to_all(x, "seq", split_axis=0, concat_axis=0, tiled=True)

    if slots == 8:
        period = total // slots
        chunks = cut_rows(period)
        lead = period // packs
        spread = exchange(deal_pieces(q_new, k_new, v_new, slots, packs))
        deal, meta, angles = lax.optimization_barrier((deal, meta, angles))
        spans = [[(lead + offset, size)] for offset, size in chunks]
        spans[0].insert(0, (0, lead))
        arrived = [exchange(route(deal, spread, span)) for span in spans]
    else:
        inverse = jnp.sum(jnp.where(deal[None, :] == slot_ids[:, None], slot_ids[None, :], 0), axis=1)

        def settle(x):
            spread = exchange(x.reshape(slots, -1, x.shape[1]))
            return exchange(jnp.take(spread, inverse, axis=0))

        period = total // 8
        chunks = cut_rows(period)
        q = settle(q_new).reshape(8, period, q_cols)
        kv = settle(jnp.concatenate([k_new, v_new], axis=1)).reshape(8, packs, period // packs, 2 * kv_cols)
        arrived = [q[:, offset : offset + size] for offset, size in chunks]
        arrived[0] = jnp.concatenate([jnp.concatenate([kv[:, b] for b in range(packs)], axis=2), arrived[0]], axis=1)
    new_k, new_v, norms = fresh_rows(meta, arrived[0], k_bias, v_bias, angles, cache_k, period // packs)
    out = None
    for i, chunk in enumerate(chunks):
        out, stat = attend(
            meta, arrived[i], q_bias, angles, caches, (new_k, new_v), norms, out, *chunk, i == 0, kv_heads
        )
        if i == 0:
            stats = [stat] + [swap_tp(stat, step) for step in range(1, lax.axis_size("tp"))]
    values = jnp.stack(stats)
    place = lax.axis_index("tp") ^ jnp.arange(len(stats), dtype=jnp.int32)
    shares = jnp.sum(values[:, 7, :], axis=1)
    shares = [jnp.sum(jnp.where(place == i, shares, 0.0)) for i in range(len(stats))]
    squares, top = functools.reduce(jnp.add, shares), jnp.max(values[:, 15, :])
    features = q_cols * lax.axis_size("tp")
    norm = jnp.sqrt(squares / features + norm_epsilon)
    return out.reshape(total, q_cols), new_k, new_v, norm.reshape(1), top.reshape(1)


def solution(mesh):
    return jax.shard_map(
        body,
        mesh=mesh,
        in_specs=(
            P("seq", "tp"),
            P("seq", "tp"),
            P("seq", "tp"),
            P("tp"),
            P("tp"),
            P("tp"),
            P("seq", "tp"),
            P("seq", "tp"),
            P(),
            P(),
        ),
        out_specs=(P("seq", "tp"), P("seq", "tp"), P("seq", "tp"), P("seq"), P("seq")),
        check_vma=False,
    )
```

profile of v0, /device:TPU:13, one launch (start us, length us, event | category | flops | bytes accessed | tf_op | source)
XLA Modules:
  0.0 224.3 jit_solution(15123489429108226115)
XLA Ops:
  0.6 4.0 %deal.1 = bf16[8,80,2048]{2,1,0:T(8,128)(2,1)} custom-call(bf16[512,2048]{1,0:T(8,128)(2,1)} %q.1, bf16[512,256]{1,0:T(8,128)(2,1)} %k.1, bf16[512,256]{1,0:T(8,128)(2,1)} %v.1), custom_call_target="tpu_custom_call" | custom-call | tf_op jit(solution)/shard_map/deal/pallas_call | solution.py:286
  4.6 0.0 copy-start.9
  4.7 5.7 %all-to-all-start = ((bf16[8,80,2048]{2,1,0:T(8,128)(2,1)}), bf16[8,80,2048]{2,1,0:T(8,128)(2,1)S(1)}, u32[]{:S(2)}, u32[]{:S(2)}) async-start(bf16[8,80,2048]{2,1,0:T(8,128)(2,1)} %deal.1), calls=%async_computation | async-start | bytes 5242880 | tf_op jit(solution)/shard_map/all_to_all | solution.py:343
  10.3 0.0 copy-done.9
  10.3 0.6 fusion.2
  11.0 0.7 pad_add_fusion.meta.refs_0_
  11.7 0.0 copy-start.4
  11.7 0.7 add_convert_fusion
  12.4 1.0 fusion
  13.4 0.2 pad_maximum_fusion
  13.6 0.0 copy-start.2
  13.6 0.0 copy-start.3
  13.6 53.7 %all-to-all-done.x = bf16[8,80,2048]{2,1,0:T(8,128)(2,1)S(1)} async-done(((bf16[8,80,2048]{2,1,0:T(8,128)(2,1)}), bf16[8,80,2048]{2,1,0:T(8,128)(2,1)S(1)}, u32[]{:S(2)}, u32[]{:S(2)}) %all-to-all-start) | async-done | bytes 2621472 | tf_op jit(solution)/shard_map/all_to_all | solution.py:343
  67.3 0.0 copy-start.6
  67.3 1.5 copy-done.6
  68.8 3.4 %route.3 = bf16[8,48,2048]{2,1,0:T(8,128)(2,1)} custom-call(s32[8]{0:T(128)} %deal.3, bf16[8,80,2048]{2,1,0:T(8,128)(2,1)} %copy-done.6), custom_call_target="tpu_custom_call" | custom-call | tf_op jit(solution)/shard_map/route/pallas_call | solution.py:313
  72.2 6.4 %all-to-all-start.2 = ((bf16[8,48,2048]{2,1,0:T(8,128)(2,1)}), bf16[8,48,2048]{2,1,0:T(8,128)(2,1)S(1)}, u32[]{:S(2)}, u32[]{:S(2)}) async-start(bf16[8,48,2048]{2,1,0:T(8,128)(2,1)} %route.3), calls=%async_computation.2 | async-start | bytes 3145728 | tf_op jit(solution)/shard_map/all_to_all | solution.py:343
  78.5 0.0 copy-start.10
  78.5 0.0 copy-start.11
  78.5 0.0 copy-start.8
  78.6 0.0 copy-start.1
  78.6 3.1 %route.2 = bf16[8,32,2048]{2,1,0:T(8,128)(2,1)} custom-call(s32[8]{0:T(128)} %deal.3, bf16[8,80,2048]{2,1,0:T(8,128)(2,1)} %copy-done.6), custom_call_target="tpu_custom_call" | custom-call | tf_op jit(solution)/shard_map/route/pallas_call | solution.py:313
  81.7 31.3 %all-to-all-done.2.arrived.refs_1_ = bf16[8,48,2048]{2,1,0:T(8,128)(2,1)S(1)} async-done(((bf16[8,48,2048]{2,1,0:T(8,128)(2,1)}), bf16[8,48,2048]{2,1,0:T(8,128)(2,1)S(1)}, u32[]{:S(2)}, u32[]{:S(2)}) %all-to-all-start.2) | async-done | bytes 1572896 | tf_op jit(solution)/shard_map/all_to_all | solution.py:343
  113.0 0.0 copy-start
  113.0 6.3 %all-to-all-start.1 = ((bf16[8,32,2048]{2,1,0:T(8,128)(2,1)}), bf16[8,32,2048]{2,1,0:T(8,128)(2,1)}, u32[]{:S(2)}, u32[]{:S(2)}) async-start(bf16[8,32,2048]{2,1,0:T(8,128)(2,1)} %route.2), calls=%async_computation.1 | async-start | bytes 2097152 | tf_op jit(solution)/shard_map/all_to_all | solution.py:343
  119.4 0.0 copy-done.10
  119.4 0.0 copy-done.11
  119.4 0.0 copy-done.8
  119.4 0.6 reshape.38.refs_2_
  120.0 0.0 copy-done.4
  120.0 0.0 copy-done.2
  120.0 0.0 copy-done.3
  120.0 0.0 copy-done.1
  120.0 2.0 fresh.1
  122.0 0.0 copy-done
  122.0 0.0 copy-start.5
  122.0 0.6 copy-done.5
  122.6 46.8 %attend.2 = (bf16[8,64,2048]{2,1,0:T(8,128)(2,1)}, f32[16,256]{1,0:T(8,128)}) custom-call(s32[2]{0:T(128)} %copy-done.4, bf16[8,48,2048]{2,1,0:T(8,128)(2,1)} %copy-done, bf16[1,2048]{1,0:T(2,128)(2,1)} %reshape.38.refs_2_, f32[512,128]{1,0:T(8,128)} %copy-done.2, f32[512,128]{1,0:T(8,128)} %copy-done.3, bf16[2048,256]{1,0:T(8,128)(2,1)} %refs_5_.3, ...), custom_call_target="tpu_custom_call" | custom-call | flops 3221225472 | bytes 2097152 | tf_op jit(solution)/shard_map/attend/pallas_call | solution.py:180
  169.5 2.7 %collective-permute-start.2 = (f32[16,256]{1,0:T(8,128)}, f32[16,256]{1,0:T(8,128)S(1)}, u32[]{:S(2)}, u32[]{:S(2)}) collective-permute-start(f32[16,256]{1,0:T(8,128)} %get-tuple-element.24), channel_id=1, source_target_pairs={{0,3},{1,2},{2,1},{3,0},{4,7},{5,6},{6,5},{7,4},{8,11},{9,10},{10,... | collective-permute-start | bytes 49160 | tf_op jit(solution)/shard_map/ppermute | solution.py:257
  172.2 0.3 collective-permute-start.1
  172.4 0.2 collective-permute-start
  172.6 0.0 all-to-all-done.1.refs_1_
  172.6 0.0 copy-start.7
  172.7 46.7 %attend.3 = (bf16[8,64,2048]{2,1,0:T(8,128)(2,1)}, f32[16,256]{1,0:T(8,128)}) custom-call(s32[2]{0:T(128)} %copy-done.4, bf16[8,32,2048]{2,1,0:T(8,128)(2,1)} %all-to-all-done.1.refs_1_, bf16[1,2048]{1,0:T(2,128)(2,1)} %reshape.38.refs_2_, f32[512,128]{1,0:T(8,128)} %copy-done.2, f32[512,128]{1,0:T(8,128)} %copy-done.3, ...), custom_call_target="tpu_custom_call", output_to_operand_aliasing={{0}: (10, {})} | custom-call | flops 3221225472 | bytes 2097152 | tf_op jit(solution)/shard_map/attend/pallas_call | solution.py:180
  219.3 0.0 collective-permute-done.2
  219.3 0.0 collective-permute-done.1
  219.3 0.0 collective-permute-done
  219.3 0.0 copy-done.7
  219.4 0.6 fusion.1
  220.0 0.7 fusion.6
  (3 shorter events, 0.0 us)
Async XLA Ops:
  4.6 5.7 %copy-start.9 = (s32[8]{0:T(128)S(1)}, s32[8]{0:T(128)}, u32[]{:S(2)}) copy-start(s32[8]{0:T(128)} %param.19) | copy-start | bytes 100
  4.7 62.6 %all-to-all-start = ((bf16[8,80,2048]{2,1,0:T(8,128)(2,1)}), bf16[8,80,2048]{2,1,0:T(8,128)(2,1)S(1)}, u32[]{:S(2)}, u32[]{:S(2)}) async-start(bf16[8,80,2048]{2,1,0:T(8,128)(2,1)} %deal.1), calls=%async_computation | async-start | bytes 5242880 | tf_op jit(solution)/shard_map/all_to_all | solution.py:343
  11.7 108.3 %copy-start.4 = (s32[2]{0:T(128)}, s32[2]{0:T(128)S(1)}, u32[]{:S(2)}) copy-start(s32[2]{0:T(128)S(1)} %pad_add_fusion.meta.refs_0_) | copy-start | bytes 28
  13.6 106.4 %copy-start.2 = (f32[512,128]{1,0:T(8,128)}, f32[512,128]{1,0:T(8,128)S(1)}, u32[]{:S(2)}) copy-start(f32[512,128]{1,0:T(8,128)S(1)} %get-tuple-element.17.cos.refs_3_) | copy-start | bytes 786436
  13.6 106.4 %copy-start.3 = (f32[512,128]{1,0:T(8,128)}, f32[512,128]{1,0:T(8,128)S(1)}, u32[]{:S(2)}) copy-start(f32[512,128]{1,0:T(8,128)S(1)} %get-tuple-element.18.sin.refs_4_) | copy-start | bytes 786436
  67.3 1.5 copy-start.6
  72.2 40.8 %all-to-all-start.2 = ((bf16[8,48,2048]{2,1,0:T(8,128)(2,1)}), bf16[8,48,2048]{2,1,0:T(8,128)(2,1)S(1)}, u32[]{:S(2)}, u32[]{:S(2)}) async-start(bf16[8,48,2048]{2,1,0:T(8,128)(2,1)} %route.3), calls=%async_computation.2 | async-start | bytes 3145728 | tf_op jit(solution)/shard_map/all_to_all | solution.py:343
  78.5 40.8 %copy-start.10 = (bf16[256]{0:T(256)(128)(2,1)S(1)}, bf16[256]{0:T(256)(128)(2,1)}, u32[]{:S(2)}) copy-start(bf16[256]{0:T(256)(128)(2,1)} %param.14) | copy-start | bytes 1540
  78.5 40.8 %copy-start.11 = (bf16[256]{0:T(256)(128)(2,1)S(1)}, bf16[256]{0:T(256)(128)(2,1)}, u32[]{:S(2)}) copy-start(bf16[256]{0:T(256)(128)(2,1)} %param.15) | copy-start | bytes 1540
  78.5 40.9 %copy-start.8 = (bf16[2048]{0:T(1024)(128)(2,1)S(1)}, bf16[2048]{0:T(1024)(128)(2,1)}, u32[]{:S(2)}) copy-start(bf16[2048]{0:T(1024)(128)(2,1)} %param.13) | copy-start | bytes 12292
  78.6 41.5 %copy-start.1 = (bf16[2048,256]{1,0:T(8,128)(2,1)S(1)}, bf16[2048,256]{1,0:T(8,128)(2,1)}, u32[]{:S(2)}) copy-start(bf16[2048,256]{1,0:T(8,128)(2,1)} %refs_5_.3) | copy-start | bytes 3145732
  113.0 9.0 %copy-start = (bf16[8,48,2048]{2,1,0:T(8,128)(2,1)}, bf16[8,48,2048]{2,1,0:T(8,128)(2,1)S(1)}, u32[]{:S(2)}) copy-start(bf16[8,48,2048]{2,1,0:T(8,128)(2,1)S(1)} %all-to-all-done.2.arrived.refs_1_) | copy-start | bytes 4718596
  113.0 59.6 %all-to-all-start.1 = ((bf16[8,32,2048]{2,1,0:T(8,128)(2,1)}), bf16[8,32,2048]{2,1,0:T(8,128)(2,1)}, u32[]{:S(2)}, u32[]{:S(2)}) async-start(bf16[8,32,2048]{2,1,0:T(8,128)(2,1)} %route.2), calls=%async_computation.1 | async-start | bytes 2097152 | tf_op jit(solution)/shard_map/all_to_all | solution.py:343
  122.0 0.6 copy-start.5
  169.5 49.8 %collective-permute-start.2 = (f32[16,256]{1,0:T(8,128)}, f32[16,256]{1,0:T(8,128)S(1)}, u32[]{:S(2)}, u32[]{:S(2)}) collective-permute-start(f32[16,256]{1,0:T(8,128)} %get-tuple-element.24), channel_id=1, source_target_pairs={{0,3},{1,2},{2,1},{3,0},{4,7},{5,6},{6,5},{7,4},{8,11},{9,10},{10,... | collective-permute-start | bytes 49160 | tf_op jit(solution)/shard_map/ppermute | solution.py:257
  172.2 47.2 %collective-permute-start.1 = (f32[16,256]{1,0:T(8,128)}, f32[16,256]{1,0:T(8,128)S(1)}, u32[]{:S(2)}, u32[]{:S(2)}) collective-permute-start(f32[16,256]{1,0:T(8,128)} %get-tuple-element.24), channel_id=1, source_target_pairs={{0,2},{1,3},{2,0},{3,1},{4,6},{5,7},{6,4},{7,5},{8,10},{9,11},{10,... | collective-permute-start | bytes 49160 | tf_op jit(solution)/shard_map/ppermute | solution.py:257
  172.4 46.9 %collective-permute-start = (f32[16,256]{1,0:T(8,128)}, f32[16,256]{1,0:T(8,128)S(1)}, u32[]{:S(2)}, u32[]{:S(2)}) collective-permute-start(f32[16,256]{1,0:T(8,128)} %get-tuple-element.24), channel_id=1, source_target_pairs={{0,1},{1,0},{2,3},{3,2},{4,5},{5,4},{6,7},{7,6},{8,9},{9,8},{10,11... | collective-permute-start | bytes 49160 | tf_op jit(solution)/shard_map/ppermute | solution.py:257
  172.6 46.7 %copy-start.7 = (f32[16,256]{1,0:T(8,128)S(1)}, f32[16,256]{1,0:T(8,128)}, u32[]{:S(2)}) copy-start(f32[16,256]{1,0:T(8,128)} %get-tuple-element.24) | copy-start | bytes 49156
where the time goes:
time: 225 us; the launch traced here: 224 us
  Pallas kernels  106 us (47%)
  waiting for transfers between devices  85 us (38%)
  starting transfers between devices  21.6 us (10%)
  other arithmetic  4.5 us (2%)
  between operations  4.48 us (2%)
  local copies, waits for them, and re-layouts  2.76 us (1%)
    pallas_call x2, Pallas kernels, attend(): pl.pallas_call(functools.partial(attend_kernel, skip=height - size, offse...  93.5 us
    all_to_all x3, waiting for transfers between devices, exchange(): return lax.all_to_all(x, 'seq', split_axis=0, concat_axis=0, tiled=True)  85 us
    all_to_all x3, starting transfers between devices, exchange(): return lax.all_to_all(x, 'seq', split_axis=0, concat_axis=0, tiled=True)  18.4 us
    pallas_call x2, Pallas kernels, route(): pl.pallas_call(functools.partial(route_kernel, spans=spans), in_specs=[SM...  6.51 us
  transfers between devices with their start and end apart: 6, of which 2 were waited for; matrix products, arithmetic and copies ran while one was open for 2% of the time, Pallas kernels for 44%

commit v1 on v0

--- a/solution.py
+++ b/solution.py
@@ -33,15 +33,15 @@
     return jnp.concatenate([x, x], axis=1)
 
 
-def attend_kernel(*refs, skip, offset, size, period, group, wide_block, block, tail):
+def attend_kernel(*refs, skip, first, group, wide_block, block, fresh_block, tail):
     meta, arrived, q_bias, cos, sin, ck, cv, nk, nv, norms = refs[:10]
     o_ref, stat, qs, m_s, l_s, acc = refs[-6:]
     length = meta[0]
     scale = HEAD**-0.5 * LOG2E
-    pieces = arrived.shape[0]
+    pieces, size = arrived.shape[0], arrived.shape[1] - skip
     rows = pieces * size
     for e in range(pieces):
-        here = slice(e * period + offset, e * period + offset + size)
+        here = slice(e * size, (e + 1) * size)
         c, s = cos[here, :], sin[here, :]
         for h in range(group):
             column = slice(h * HEAD, (h + 1) * HEAD)
@@ -65,10 +65,8 @@
     cached = (length + block - 1) // block
 
     def causal(heads, width):
-        shape = (heads * pieces, size, width)
-        piece = lax.broadcasted_iota(jnp.int32, shape, 0) % pieces
-        row = (piece * period + lax.broadcasted_iota(jnp.int32, shape, 1)).reshape(heads * rows, width)
-        return lax.broadcasted_iota(jnp.int32, (heads * rows, width), 1) - row <= offset
+        row = lax.broadcasted_iota(jnp.int32, (heads, rows, width), 1).reshape(heads * rows, width)
+        return lax.broadcasted_iota(jnp.int32, (heads * rows, width), 1) - row <= first
 
     @pl.when(bound <= SAFE * SAFE)
     def _():
@@ -92,7 +90,7 @@
 
         lax.fori_loop(0, whole, full, 0)
         lax.fori_loop(rest, cached, partial, 0)
-        add(nk[...], nv[...], causal(group, nk.shape[0]))
+        add(nk[...], nv[...], causal(group, fresh_block))
 
     @pl.when(bound > SAFE * SAFE)
     def _():
@@ -123,13 +121,13 @@
             return carry
 
         lax.fori_loop(0, cached, step, 0)
-        online(nk[...], nv[...], causal(1, nk.shape[0]))
+        online(nk[...], nv[...], causal(1, fresh_block))
 
     squares = jnp.zeros((8, HEAD), f32)
     for h in range(group):
         at = slice(h * rows, (h + 1) * rows)
         mixture = acc[at, :] / jnp.sum(l_s[at, :], axis=1, keepdims=True)
-        o_ref[:, :, h * HEAD : (h + 1) * HEAD] = mixture.astype(bf16).reshape(pieces, size, HEAD)
+        o_ref[:, h * HEAD : (h + 1) * HEAD] = mixture.astype(bf16)
         end = mixture[rows - 8 :, :]
         squares = squares + end * end
     if tail:
@@ -150,25 +148,26 @@
         stat[...] = jnp.zeros_like(stat)
 
 
-def attend(meta, arrived, bias, angles, caches, news, norms, out, offset, size, tail, kv_heads):
+def attend(meta, arrived, bias, angles, caches, news, norms, out, first, rows, tail, kv_heads):
     pieces, height, q_cols = arrived.shape
-    rows = pieces * size
+    size = rows // pieces
     group = q_cols // HEAD // kv_heads
     wide = group * HEAD
     fresh, cache_rows = news[0].shape[0], caches[0].shape[0]
-    period = fresh // pieces
+    fresh_block = min(fresh, -(-(first + rows) // 256) * 256)
     wide_block, block = math.gcd(1024, cache_rows), math.gcd(512, cache_rows)
     column = lambda n, width: pl.BlockSpec((n, width), lambda g, m: (0, g))
-    table = pl.BlockSpec((fresh, HEAD), lambda g, m: (0, 0))
+    table = pl.BlockSpec((rows, HEAD), lambda g, m: (first // rows, 0))
     given = [] if out is None else [out]
     spec = pltpu.PrefetchScalarGridSpec(
         num_scalar_prefetch=1,
         grid=(kv_heads,),
         in_specs=[
             pl.BlockSpec((pieces, height, wide), lambda g, m: (0, 0, g)), column(1, wide), table, table,
-            column(cache_rows, HEAD), column(cache_rows, HEAD), column(fresh, HEAD), column(fresh, HEAD), column(8, HEAD),
+            column(cache_rows, HEAD), column(cache_rows, HEAD),
+            column(fresh_block, HEAD), column(fresh_block, HEAD), column(8, HEAD),
         ] + [ANY] * len(given),
-        out_specs=[pl.BlockSpec((pieces, size, wide), lambda g, m: (0, offset // size, g)), column(16, HEAD)],
+        out_specs=[pl.BlockSpec((rows, wide), lambda g, m: (first // rows, g)), column(16, HEAD)],
         scratch_shapes=[
             pltpu.VMEM((group * rows, 2 * HEAD), bf16),
             pltpu.VMEM((group * rows, HEAD), f32),
@@ -179,12 +178,12 @@
     work = kv_heads * group * rows * (cache_rows // 2 + fresh)
     return pl.pallas_call(
         functools.partial(
-            attend_kernel, skip=height - size, offset=offset, size=size, period=period, group=group,
-            wide_block=wide_block, block=block, tail=tail,
+            attend_kernel, skip=height - size, first=first, group=group,
+            wide_block=wide_block, block=block, fresh_block=fresh_block, tail=tail,
         ),
         grid_spec=spec,
         out_shape=[
-            jax.ShapeDtypeStruct((pieces, period, q_cols), bf16),
+            jax.ShapeDtypeStruct((fresh, q_cols), bf16),
             jax.ShapeDtypeStruct((16, kv_heads * HEAD), f32),
         ],
         input_output_aliases={10: 0} if given else {},
@@ -257,72 +256,85 @@
     return lax.ppermute(pair, "tp", [(i, i ^ step) for i in range(size)])
 
 
-def run_copies(copies):
-    for copy in copies:
-        copy.start()
-    for copy in copies:
-        copy.wait()
-
-
-def deal_kernel(q, k, v, out, held, sems, *, packs):
+def pass_on(into, back):
+    for group in into:
+        for copy in group:
+            copy.start()
+    for group, after in zip(into, back):
+        for copy in group:
+            copy.wait()
+        for copy in after:
+            copy.start()
+    for after in back:
+        for copy in after:
+            copy.wait()
+
+
+def deal_kernel(q, k, v, out, held, sems, out_sems, *, chunks, packs):
     pieces, height, _ = held.shape
-    size = q.shape[0] // pieces
-    kv_size = height - size
-    copies = []
+    kv_size = height - sum(rows for _, rows in chunks) // pieces
+    into = []
     for e in range(pieces):
-        copies.append((q.at[pl.ds(e * size, size)], held.at[e, pl.ds(kv_size, size)]))
+        copies, base = [], kv_size
+        for first, rows in chunks:
+            size = rows // pieces
+            copies.append((q.at[pl.ds(first + e * size, size)], held.at[e, pl.ds(base, size)]))
+            base += size
         for b in range(packs):
             rows = pl.ds((e * packs + b) * kv_size, kv_size)
             for n, x in enumerate((k, v)):
                 width = x.shape[1]
                 copies.append((x.at[rows], held.at[e, pl.ds(0, kv_size), pl.ds((2 * b + n) * width, width)]))
-    run_copies([pltpu.make_async_copy(a, b, sems.at[n]) for n, (a, b) in enumerate(copies)])
-    run_copies([pltpu.make_async_copy(held, out, sems.at[0])])
-
-
-def deal_pieces(q, k, v, pieces, packs):
+        into.append([pltpu.make_async_copy(a, b, sems.at[e * len(copies) + n]) for n, (a, b) in enumerate(copies)])
+    pass_on(into, [[pltpu.make_async_copy(held.at[e], out.at[e], out_sems.at[e])] for e in range(pieces)])
+
+
+def deal_pieces(q, k, v, pieces, packs, chunks):
     total, q_cols = q.shape
-    shape = (pieces, total // pieces + total // pieces // packs, q_cols)
+    shape = (pieces, total // pieces // packs + sum(rows for _, rows in chunks) // pieces, q_cols)
     return pl.pallas_call(
-        functools.partial(deal_kernel, packs=packs),
+        functools.partial(deal_kernel, chunks=chunks, packs=packs),
         in_specs=[ANY] * 3,
         out_specs=ANY,
         out_shape=jax.ShapeDtypeStruct(shape, bf16),
-        scratch_shapes=[pltpu.VMEM(shape, bf16), pltpu.SemaphoreType.DMA((pieces * (1 + 2 * packs),))],
+        scratch_shapes=[
+            pltpu.VMEM(shape, bf16),
+            pltpu.SemaphoreType.DMA((pieces * (len(chunks) + 2 * packs),)),
+            pltpu.SemaphoreType.DMA((pieces,)),
+        ],
         compiler_params=pltpu.CompilerParams(vmem_limit_bytes=60 << 20),
         name="deal",
     )(q, k, v)
 
 
-def route_kernel(deal, x, out, held, sems, *, spans):
+def route_kernel(deal, x, out, held, sems, out_sems, *, span):
     slots = x.shape[0]
-    into, back = [], []
-    for s in range(slots):
-        base = 0
-        for n, (offset, size) in enumerate(spans):
-            into.append(pltpu.make_async_copy(x.at[s, pl.ds(offset, size)], held.at[s, pl.ds(base, size)], sems.at[n, s]))
-            base += size
-        back.append(pltpu.make_async_copy(held.at[s], out.at[deal[s]], sems.at[0, s]))
-    run_copies(into)
-    run_copies(back)
-
-
-def route(deal, x, spans):
+    pass_on(
+        [[pltpu.make_async_copy(x.at[s, pl.ds(*span)], held.at[s], sems.at[s])] for s in range(slots)],
+        [[pltpu.make_async_copy(held.at[s], out.at[deal[s]], out_sems.at[s])] for s in range(slots)],
+    )
+
+
+def route(deal, x, span):
     slots, _, q_cols = x.shape
-    shape = (slots, sum(size for _, size in spans), q_cols)
+    shape = (slots, span[1], q_cols)
     return pl.pallas_call(
-        functools.partial(route_kernel, spans=spans),
+        functools.partial(route_kernel, span=span),
         in_specs=[SMEM, ANY],
         out_specs=ANY,
         out_shape=jax.ShapeDtypeStruct(shape, bf16),
-        scratch_shapes=[pltpu.VMEM(shape, bf16), pltpu.SemaphoreType.DMA((len(spans), slots))],
+        scratch_shapes=[
+            pltpu.VMEM(shape, bf16),
+            pltpu.SemaphoreType.DMA((slots,)),
+            pltpu.SemaphoreType.DMA((slots,)),
+        ],
         compiler_params=pltpu.CompilerParams(vmem_limit_bytes=60 << 20),
         name="route",
     )(deal, x)
 
 
-def cut_rows(period):
-    return [(period // 2, period // 2), (0, period // 2)]
+def cut_rows(total):
+    return [(total // 2, total // 2), (0, total // 2)]
 
 
 def body(q_new, k_new, v_new, q_bias, k_bias, v_bias, cache_k, cache_v, deal, cache_len):
@@ -342,14 +354,17 @@
     def exchange(x):
         return lax.all_to_all(x, "seq", split_axis=0, concat_axis=0, tiled=True)
 
-    if slots == 8:
-        period = total // slots
-        chunks = cut_rows(period)
-        lead = period // packs
-        spread = exchange(deal_pieces(q_new, k_new, v_new, slots, packs))
-        deal, meta, angles = lax.optimization_barrier((deal, meta, angles))
-        spans = [[(lead + offset, size)] for offset, size in chunks]
-        spans[0].insert(0, (0, lead))
+    pieces = 8
+    lead = total // pieces // packs
+    chunks = cut_rows(total)
+    if slots == pieces:
+        spread = exchange(deal_pieces(q_new, k_new, v_new, pieces, packs, chunks))
+        deal, meta, angles, q_bias, k_bias, v_bias = lax.optimization_barrier(
+            (deal, meta, angles, q_bias, k_bias, v_bias)
+        )
+        heights = [rows // pieces for _, rows in chunks]
+        heights[0] += lead
+        spans = [(sum(heights[:i]), heights[i]) for i in range(len(heights))]
         arrived = [exchange(route(deal, spread, span)) for span in spans]
     else:
         inverse = jnp.sum(jnp.where(deal[None, :] == slot_ids[:, None], slot_ids[None, :], 0), axis=1)
@@ -358,13 +373,11 @@
             spread = exchange(x.reshape(slots, -1, x.shape[1]))
             return exchange(jnp.take(spread, inverse, axis=0))
 
-        period = total // 8
-        chunks = cut_rows(period)
-        q = settle(q_new).reshape(8, period, q_cols)
-        kv = settle(jnp.concatenate([k_new, v_new], axis=1)).reshape(8, packs, period // packs, 2 * kv_cols)
-        arrived = [q[:, offset : offset + size] for offset, size in chunks]
+        q = settle(q_new).reshape(total, q_cols)
+        kv = settle(jnp.concatenate([k_new, v_new], axis=1)).reshape(pieces, packs, lead, 2 * kv_cols)
+        arrived = [q[first : first + rows].reshape(pieces, -1, q_cols) for first, rows in chunks]
         arrived[0] = jnp.concatenate([jnp.concatenate([kv[:, b] for b in range(packs)], axis=2), arrived[0]], axis=1)
-    new_k, new_v, norms = fresh_rows(meta, arrived[0], k_bias, v_bias, angles, cache_k, period // packs)
+    new_k, new_v, norms = fresh_rows(meta, arrived[0], k_bias, v_bias, angles, cache_k, lead)
     out = None
     for i, chunk in enumerate(chunks):
         out, stat = attend(

time: 225 us -> 223 us (level)
  no operation moved by 1% of the time
where the time goes in v1:
time: 223 us; the launch traced here: 222 us
  Pallas kernels  104 us (47%)
  waiting for transfers between devices  84.6 us (38%)
  starting transfers between devices  21.7 us (10%)
  other arithmetic  4.5 us (2%)
  between operations  4.49 us (2%)
  local copies, waits for them, and re-layouts  2.77 us (1%)
    pallas_call x2, Pallas kernels, attend(): pl.pallas_call(functools.partial(attend_kernel, skip=height - size, first...  92.5 us
    all_to_all x3, waiting for transfers between devices, exchange(): return lax.all_to_all(x, 'seq', split_axis=0, concat_axis=0, tiled=True)  84.6 us
    all_to_all x3, starting transfers between devices, exchange(): return lax.all_to_all(x, 'seq', split_axis=0, concat_axis=0, tiled=True)  18.5 us
    pallas_call x2, Pallas kernels, route(): pl.pallas_call(functools.partial(route_kernel, span=span), in_specs=[SMEM...  5.88 us
  transfers between devices with their start and end apart: 6, of which 2 were waited for; matrix products, arithmetic and copies ran while one was open for 2% of the time, Pallas kernels for 44%

profile of v1, /device:TPU:13, one launch (start us, length us, event | category | flops | bytes accessed | tf_op | source)
XLA Modules:
  0.0 221.9 jit_solution(13410614230551013637)
XLA Ops:
  0.6 3.5 %deal.1 = bf16[8,80,2048]{2,1,0:T(8,128)(2,1)} custom-call(bf16[512,2048]{1,0:T(8,128)(2,1)} %q.1, bf16[512,256]{1,0:T(8,128)(2,1)} %k.1, bf16[512,256]{1,0:T(8,128)(2,1)} %v.1), custom_call_target="tpu_custom_call" | custom-call | tf_op jit(solution)/shard_map/deal/pallas_call | solution.py:295
  4.1 0.0 copy-start.9
  4.1 0.0 copy-start.10
  4.1 0.0 copy-start.8
  4.2 0.0 copy-start.11
  4.2 5.8 %all-to-all-start = ((bf16[8,80,2048]{2,1,0:T(8,128)(2,1)}), bf16[8,80,2048]{2,1,0:T(8,128)(2,1)S(1)}, u32[]{:S(2)}, u32[]{:S(2)}) async-start(bf16[8,80,2048]{2,1,0:T(8,128)(2,1)} %deal.1), calls=%async_computation | async-start | bytes 5242880 | tf_op jit(solution)/shard_map/all_to_all | solution.py:355
  10.0 0.0 copy-done.9
  10.0 0.0 copy-done.10
  10.0 0.0 copy-done.8
  10.0 0.6 reshape.35.refs_2_
  10.6 0.0 copy-done.11
  10.6 0.6 fusion.2
  11.3 0.7 pad_add_fusion.meta.refs_0_
  12.0 0.0 copy-start.4
  12.0 0.7 add_convert_fusion
  12.6 1.0 fusion
  13.6 0.2 pad_maximum_fusion
  13.9 0.0 copy-start.2
  13.9 0.0 copy-start.3
  13.9 53.0 %all-to-all-done.x = bf16[8,80,2048]{2,1,0:T(8,128)(2,1)S(1)} async-done(((bf16[8,80,2048]{2,1,0:T(8,128)(2,1)}), bf16[8,80,2048]{2,1,0:T(8,128)(2,1)S(1)}, u32[]{:S(2)}, u32[]{:S(2)}) %all-to-all-start) | async-done | bytes 2621472 | tf_op jit(solution)/shard_map/all_to_all | solution.py:355
  66.9 0.0 copy-start.6
  66.9 1.5 copy-done.6
  68.4 3.0 %route.3 = bf16[8,48,2048]{2,1,0:T(8,128)(2,1)} custom-call(s32[8]{0:T(128)} %deal.3, bf16[8,80,2048]{2,1,0:T(8,128)(2,1)} %copy-done.6), custom_call_target="tpu_custom_call" | custom-call | tf_op jit(solution)/shard_map/route/pallas_call | solution.py:321
  71.4 6.4 %all-to-all-start.2 = ((bf16[8,48,2048]{2,1,0:T(8,128)(2,1)}), bf16[8,48,2048]{2,1,0:T(8,128)(2,1)S(1)}, u32[]{:S(2)}, u32[]{:S(2)}) async-start(bf16[8,48,2048]{2,1,0:T(8,128)(2,1)} %route.3), calls=%async_computation.2 | async-start | bytes 3145728 | tf_op jit(solution)/shard_map/all_to_all | solution.py:355
  77.8 0.0 copy-start.1
  77.8 2.9 %route.2 = bf16[8,32,2048]{2,1,0:T(8,128)(2,1)} custom-call(s32[8]{0:T(128)} %deal.3, bf16[8,80,2048]{2,1,0:T(8,128)(2,1)} %copy-done.6), custom_call_target="tpu_custom_call" | custom-call | tf_op jit(solution)/shard_map/route/pallas_call | solution.py:321
  80.7 31.5 %all-to-all-done.2.arrived.refs_1_ = bf16[8,48,2048]{2,1,0:T(8,128)(2,1)S(1)} async-done(((bf16[8,48,2048]{2,1,0:T(8,128)(2,1)}), bf16[8,48,2048]{2,1,0:T(8,128)(2,1)S(1)}, u32[]{:S(2)}, u32[]{:S(2)}) %all-to-all-start.2) | async-done | bytes 1572896 | tf_op jit(solution)/shard_map/all_to_all | solution.py:355
  112.2 0.0 copy-start
  112.2 6.3 %all-to-all-start.1 = ((bf16[8,32,2048]{2,1,0:T(8,128)(2,1)}), bf16[8,32,2048]{2,1,0:T(8,128)(2,1)}, u32[]{:S(2)}, u32[]{:S(2)}) async-start(bf16[8,32,2048]{2,1,0:T(8,128)(2,1)} %route.2), calls=%async_computation.1 | async-start | bytes 2097152 | tf_op jit(solution)/shard_map/all_to_all | solution.py:355
  118.6 0.0 copy-done.4
  118.6 0.0 copy-done.2
  118.6 0.0 copy-done.3
  118.6 0.0 copy-done.1
  118.6 2.0 fresh.1
  120.6 0.0 copy-done
  120.6 0.0 copy-start.5
  120.6 0.6 copy-done.5
  121.2 46.7 %attend.2 = (bf16[512,2048]{1,0:T(8,128)(2,1)}, f32[16,256]{1,0:T(8,128)}) custom-call(s32[2]{0:T(128)} %copy-done.4, bf16[8,48,2048]{2,1,0:T(8,128)(2,1)} %copy-done, bf16[1,2048]{1,0:T(2,128)(2,1)} %reshape.35.refs_2_, f32[512,128]{1,0:T(8,128)} %copy-done.2, f32[512,128]{1,0:T(8,128)} %copy-done.3, bf16[2048,256]{1,0:T(8,128)(2,1)} %refs_5_.3, ...), custom_call_target="tpu_custom_call" | custom-call | flops 3221225472 | bytes 2097152 | tf_op jit(solution)/shard_map/attend/pallas_call | solution.py:179
  168.0 2.7 %collective-permute-start.2 = (f32[16,256]{1,0:T(8,128)}, f32[16,256]{1,0:T(8,128)S(1)}, u32[]{:S(2)}, u32[]{:S(2)}) collective-permute-start(f32[16,256]{1,0:T(8,128)} %get-tuple-element.30), channel_id=1, source_target_pairs={{0,3},{1,2},{2,1},{3,0},{4,7},{5,6},{6,5},{7,4},{8,11},{9,10},{10,... | collective-permute-start | bytes 49160 | tf_op jit(solution)/shard_map/ppermute | solution.py:256
  170.7 0.3 collective-permute-start.1
  170.9 0.2 collective-permute-start
  171.1 0.0 all-to-all-done.1.refs_1_
  171.1 0.0 copy-start.7
  171.1 45.8 %attend.3 = (bf16[512,2048]{1,0:T(8,128)(2,1)}, f32[16,256]{1,0:T(8,128)}) custom-call(s32[2]{0:T(128)} %copy-done.4, bf16[8,32,2048]{2,1,0:T(8,128)(2,1)} %all-to-all-done.1.refs_1_, bf16[1,2048]{1,0:T(2,128)(2,1)} %reshape.35.refs_2_, f32[512,128]{1,0:T(8,128)} %copy-done.2, f32[512,128]{1,0:T(8,128)} %copy-done.3, ...), custom_call_target="tpu_custom_call", output_to_operand_aliasing={{0}: (10, {})} | custom-call | flops 3221225472 | bytes 2097152 | tf_op jit(solution)/shard_map/attend/pallas_call | solution.py:179
  216.9 0.0 collective-permute-done.2
  216.9 0.0 collective-permute-done.1
  216.9 0.0 collective-permute-done
  217.0 0.0 copy-done.7
  217.0 0.6 fusion.1
  217.6 0.7 fusion.6
  (3 shorter events, 0.0 us)
Async XLA Ops:
  4.1 5.9 %copy-start.9 = (bf16[256]{0:T(256)(128)(2,1)S(1)}, bf16[256]{0:T(256)(128)(2,1)}, u32[]{:S(2)}) copy-start(bf16[256]{0:T(256)(128)(2,1)} %param.14) | copy-start | bytes 1540
  4.1 5.9 %copy-start.10 = (bf16[256]{0:T(256)(128)(2,1)S(1)}, bf16[256]{0:T(256)(128)(2,1)}, u32[]{:S(2)}) copy-start(bf16[256]{0:T(256)(128)(2,1)} %param.15) | copy-start | bytes 1540
  4.1 5.9 %copy-start.8 = (bf16[2048]{0:T(1024)(128)(2,1)S(1)}, bf16[2048]{0:T(1024)(128)(2,1)}, u32[]{:S(2)}) copy-start(bf16[2048]{0:T(1024)(128)(2,1)} %param.13) | copy-start | bytes 12292
  4.2 6.5 %copy-start.11 = (s32[8]{0:T(128)S(1)}, s32[8]{0:T(128)}, u32[]{:S(2)}) copy-start(s32[8]{0:T(128)} %param.19) | copy-start | bytes 100
  4.2 62.8 %all-to-all-start = ((bf16[8,80,2048]{2,1,0:T(8,128)(2,1)}), bf16[8,80,2048]{2,1,0:T(8,128)(2,1)S(1)}, u32[]{:S(2)}, u32[]{:S(2)}) async-start(bf16[8,80,2048]{2,1,0:T(8,128)(2,1)} %deal.1), calls=%async_computation | async-start | bytes 5242880 | tf_op jit(solution)/shard_map/all_to_all | solution.py:355
  12.0 106.6 %copy-start.4 = (s32[2]{0:T(128)}, s32[2]{0:T(128)S(1)}, u32[]{:S(2)}) copy-start(s32[2]{0:T(128)S(1)} %pad_add_fusion.meta.refs_0_) | copy-start | bytes 28
  13.9 104.7 %copy-start.2 = (f32[512,128]{1,0:T(8,128)}, f32[512,128]{1,0:T(8,128)S(1)}, u32[]{:S(2)}) copy-start(f32[512,128]{1,0:T(8,128)S(1)} %get-tuple-element.21.cos.refs_3_) | copy-start | bytes 786436
  13.9 104.7 %copy-start.3 = (f32[512,128]{1,0:T(8,128)}, f32[512,128]{1,0:T(8,128)S(1)}, u32[]{:S(2)}) copy-start(f32[512,128]{1,0:T(8,128)S(1)} %get-tuple-element.22.sin.refs_4_) | copy-start | bytes 786436
  66.9 1.5 copy-start.6
  71.4 40.8 %all-to-all-start.2 = ((bf16[8,48,2048]{2,1,0:T(8,128)(2,1)}), bf16[8,48,2048]{2,1,0:T(8,128)(2,1)S(1)}, u32[]{:S(2)}, u32[]{:S(2)}) async-start(bf16[8,48,2048]{2,1,0:T(8,128)(2,1)} %route.3), calls=%async_computation.2 | async-start | bytes 3145728 | tf_op jit(solution)/shard_map/all_to_all | solution.py:355
  77.8 40.8 %copy-start.1 = (bf16[2048,256]{1,0:T(8,128)(2,1)S(1)}, bf16[2048,256]{1,0:T(8,128)(2,1)}, u32[]{:S(2)}) copy-start(bf16[2048,256]{1,0:T(8,128)(2,1)} %refs_5_.3) | copy-start | bytes 3145732
  112.2 8.4 %copy-start = (bf16[8,48,2048]{2,1,0:T(8,128)(2,1)}, bf16[8,48,2048]{2,1,0:T(8,128)(2,1)S(1)}, u32[]{:S(2)}) copy-start(bf16[8,48,2048]{2,1,0:T(8,128)(2,1)S(1)} %all-to-all-done.2.arrived.refs_1_) | copy-start | bytes 4718596
  112.2 58.9 %all-to-all-start.1 = ((bf16[8,32,2048]{2,1,0:T(8,128)(2,1)}), bf16[8,32,2048]{2,1,0:T(8,128)(2,1)}, u32[]{:S(2)}, u32[]{:S(2)}) async-start(bf16[8,32,2048]{2,1,0:T(8,128)(2,1)} %route.2), calls=%async_computation.1 | async-start | bytes 2097152 | tf_op jit(solution)/shard_map/all_to_all | solution.py:355
  120.6 0.6 copy-start.5
  168.0 49.0 %collective-permute-start.2 = (f32[16,256]{1,0:T(8,128)}, f32[16,256]{1,0:T(8,128)S(1)}, u32[]{:S(2)}, u32[]{:S(2)}) collective-permute-start(f32[16,256]{1,0:T(8,128)} %get-tuple-element.30), channel_id=1, source_target_pairs={{0,3},{1,2},{2,1},{3,0},{4,7},{5,6},{6,5},{7,4},{8,11},{9,10},{10,... | collective-permute-start | bytes 49160 | tf_op jit(solution)/shard_map/ppermute | solution.py:256
  170.7 46.3 %collective-permute-start.1 = (f32[16,256]{1,0:T(8,128)}, f32[16,256]{1,0:T(8,128)S(1)}, u32[]{:S(2)}, u32[]{:S(2)}) collective-permute-start(f32[16,256]{1,0:T(8,128)} %get-tuple-element.30), channel_id=1, source_target_pairs={{0,2},{1,3},{2,0},{3,1},{4,6},{5,7},{6,4},{7,5},{8,10},{9,11},{10,... | collective-permute-start | bytes 49160 | tf_op jit(solution)/shard_map/ppermute | solution.py:256
  170.9 46.0 %collective-permute-start = (f32[16,256]{1,0:T(8,128)}, f32[16,256]{1,0:T(8,128)S(1)}, u32[]{:S(2)}, u32[]{:S(2)}) collective-permute-start(f32[16,256]{1,0:T(8,128)} %get-tuple-element.30), channel_id=1, source_target_pairs={{0,1},{1,0},{2,3},{3,2},{4,5},{5,4},{6,7},{7,6},{8,9},{9,8},{10,11... | collective-permute-start | bytes 49160 | tf_op jit(solution)/shard_map/ppermute | solution.py:256
  171.1 45.8 %copy-start.7 = (f32[16,256]{1,0:T(8,128)S(1)}, f32[16,256]{1,0:T(8,128)}, u32[]{:S(2)}) copy-start(f32[16,256]{1,0:T(8,128)} %get-tuple-element.30) | copy-start | bytes 49156

commit v2 on v1

--- a/solution.py
+++ b/solution.py
@@ -155,7 +155,7 @@
     wide = group * HEAD
     fresh, cache_rows = news[0].shape[0], caches[0].shape[0]
     fresh_block = min(fresh, -(-(first + rows) // 256) * 256)
-    wide_block, block = math.gcd(1024, cache_rows), math.gcd(512, cache_rows)
+    wide_block, block = math.gcd(2048, cache_rows), math.gcd(512, cache_rows)
     column = lambda n, width: pl.BlockSpec((n, width), lambda g, m: (0, g))
     table = pl.BlockSpec((rows, HEAD), lambda g, m: (first // rows, 0))
     given = [] if out is None else [out]
@@ -337,6 +337,18 @@
     return [(total // 2, total // 2), (0, total // 2)]
 
 
+def finish(stat, q_cols):
+    stats = [stat] + [swap_tp(stat, step) for step in range(1, lax.axis_size("tp"))]
+    values = jnp.stack(stats)
+    place = lax.axis_index("tp") ^ jnp.arange(len(stats), dtype=jnp.int32)
+    shares = jnp.sum(values[:, 7, :], axis=1)
+    shares = [jnp.sum(jnp.where(place == i, shares, 0.0)) for i in range(len(stats))]
+    squares, top = functools.reduce(jnp.add, shares), jnp.max(values[:, 15, :])
+    features = q_cols * lax.axis_size("tp")
+    norm = jnp.sqrt(squares / features + norm_epsilon)
+    return norm, top
+
+
 def body(q_new, k_new, v_new, q_bias, k_bias, v_bias, cache_k, cache_v, deal, cache_len):
     slots = lax.axis_size("seq")
     own = lax.axis_index("seq").astype(jnp.int32)
@@ -384,14 +396,8 @@
             meta, arrived[i], q_bias, angles, caches, (new_k, new_v), norms, out, *chunk, i == 0, kv_heads
         )
         if i == 0:
-            stats = [stat] + [swap_tp(stat, step) for step in range(1, lax.axis_size("tp"))]
-    values = jnp.stack(stats)
-    place = lax.axis_index("tp") ^ jnp.arange(len(stats), dtype=jnp.int32)
-    shares = jnp.sum(values[:, 7, :], axis=1)
-    shares = [jnp.sum(jnp.where(place == i, shares, 0.0)) for i in range(len(stats))]
-    squares, top = functools.reduce(jnp.add, shares), jnp.max(values[:, 15, :])
-    features = q_cols * lax.axis_size("tp")
-    norm = jnp.sqrt(squares / features + norm_epsilon)
+            norm, top = finish(stat, q_cols)
+            meta, norm, top = lax.optimization_barrier((meta, norm, top))
     return out.reshape(total, q_cols), new_k, new_v, norm.reshape(1), top.reshape(1)
 
 

time: 223 us -> 226 us (1.013)
  the two profiles are of different devices: /device:TPU:13 before, /device:TPU:21 now
where the time goes in v2:
time: 226 us; the launch traced here: 225 us
  Pallas kernels  104 us (46%)
  waiting for transfers between devices  85 us (38%)
  starting transfers between devices  23.5 us (10%)
  other arithmetic  5.32 us (2%)
  between operations  4.48 us (2%)
  local copies, waits for them, and re-layouts  2.77 us (1%)
    pallas_call x2, Pallas kernels, attend(): pl.pallas_call(functools.partial(attend_kernel, skip=height - size, first...  92.4 us
    all_to_all x3, waiting for transfers between devices, exchange(): return lax.all_to_all(x, 'seq', split_axis=0, concat_axis=0, tiled=True)  82.7 us
    all_to_all x3, starting transfers between devices, exchange(): return lax.all_to_all(x, 'seq', split_axis=0, concat_axis=0, tiled=True)  20.3 us
    pallas_call x2, Pallas kernels, route(): pl.pallas_call(functools.partial(route_kernel, span=span), in_specs=[SMEM...  5.87 us
  transfers between devices with their start and end apart: 6, of which 4 were waited for; matrix products, arithmetic and copies ran while one was open for 3% of the time, Pallas kernels for 23%

profile of v2, /device:TPU:21, one launch (start us, length us, event | category | flops | bytes accessed | tf_op | source)
XLA Modules:
  0.0 224.9 jit_solution(8097392974620231269)
XLA Ops:
  0.6 3.5 %deal.1 = bf16[8,80,2048]{2,1,0:T(8,128)(2,1)} custom-call(bf16[512,2048]{1,0:T(8,128)(2,1)} %q.1, bf16[512,256]{1,0:T(8,128)(2,1)} %k.1, bf16[512,256]{1,0:T(8,128)(2,1)} %v.1), custom_call_target="tpu_custom_call" | custom-call | tf_op jit(solution)/shard_map/deal/pallas_call | solution.py:295
  4.1 0.0 copy-start.8
  4.1 0.0 copy-start.9
  4.1 0.0 copy-start.7
  4.2 0.0 copy-start.10
  4.2 5.7 %all-to-all-start = ((bf16[8,80,2048]{2,1,0:T(8,128)(2,1)}), bf16[8,80,2048]{2,1,0:T(8,128)(2,1)S(1)}, u32[]{:S(2)}, u32[]{:S(2)}) async-start(bf16[8,80,2048]{2,1,0:T(8,128)(2,1)} %deal.1), calls=%async_computation | async-start | bytes 5242880 | tf_op jit(solution)/shard_map/all_to_all | solution.py:367
  9.9 0.0 copy-done.8
  9.9 0.0 copy-done.9
  9.9 0.0 copy-done.7
  9.9 0.6 reshape.35.refs_2_
  10.5 0.0 copy-done.10
  10.5 0.6 fusion.2
  11.2 0.7 pad_add_fusion.meta.refs_0_
  11.9 0.0 copy-start.4
  11.9 0.7 add_convert_fusion
  12.5 1.0 fusion
  13.5 0.2 pad_maximum_fusion
  13.7 0.0 copy-start.2
  13.7 0.0 copy-start.3
  13.8 52.1 %all-to-all-done.x = bf16[8,80,2048]{2,1,0:T(8,128)(2,1)S(1)} async-done(((bf16[8,80,2048]{2,1,0:T(8,128)(2,1)}), bf16[8,80,2048]{2,1,0:T(8,128)(2,1)S(1)}, u32[]{:S(2)}, u32[]{:S(2)}) %all-to-all-start) | async-done | bytes 2621472 | tf_op jit(solution)/shard_map/all_to_all | solution.py:367
  65.8 0.0 copy-start.6
  65.9 1.5 copy-done.6
  67.4 3.0 %route.2 = bf16[8,48,2048]{2,1,0:T(8,128)(2,1)} custom-call(s32[8]{0:T(128)} %deal.3, bf16[8,80,2048]{2,1,0:T(8,128)(2,1)} %copy-done.6), custom_call_target="tpu_custom_call" | custom-call | tf_op jit(solution)/shard_map/route/pallas_call | solution.py:321
  70.3 7.3 %all-to-all-start.1 = ((bf16[8,48,2048]{2,1,0:T(8,128)(2,1)}), bf16[8,48,2048]{2,1,0:T(8,128)(2,1)S(1)}, u32[]{:S(2)}, u32[]{:S(2)}) async-start(bf16[8,48,2048]{2,1,0:T(8,128)(2,1)} %route.2), calls=%async_computation.1 | async-start | bytes 3145728 | tf_op jit(solution)/shard_map/all_to_all | solution.py:367
  77.7 0.0 copy-start.1
  77.7 2.9 %route.3 = bf16[8,32,2048]{2,1,0:T(8,128)(2,1)} custom-call(s32[8]{0:T(128)} %deal.3, bf16[8,80,2048]{2,1,0:T(8,128)(2,1)} %copy-done.6), custom_call_target="tpu_custom_call" | custom-call | tf_op jit(solution)/shard_map/route/pallas_call | solution.py:321
  80.6 30.6 %all-to-all-done.1.arrived.refs_1_ = bf16[8,48,2048]{2,1,0:T(8,128)(2,1)S(1)} async-done(((bf16[8,48,2048]{2,1,0:T(8,128)(2,1)}), bf16[8,48,2048]{2,1,0:T(8,128)(2,1)S(1)}, u32[]{:S(2)}, u32[]{:S(2)}) %all-to-all-start.1) | async-done | bytes 1572896 | tf_op jit(solution)/shard_map/all_to_all | solution.py:367
  111.2 0.0 copy-start
  111.2 7.3 %all-to-all-start.2 = ((bf16[8,32,2048]{2,1,0:T(8,128)(2,1)}), bf16[8,32,2048]{2,1,0:T(8,128)(2,1)}, u32[]{:S(2)}, u32[]{:S(2)}) async-start(bf16[8,32,2048]{2,1,0:T(8,128)(2,1)} %route.3), calls=%async_computation.2 | async-start | bytes 2097152 | tf_op jit(solution)/shard_map/all_to_all | solution.py:367
  118.5 0.0 copy-done.4
  118.5 0.0 copy-done.2
  118.5 0.0 copy-done.3
  118.5 0.0 copy-done.1
  118.5 2.0 fresh.1
  120.5 0.0 copy-done
  120.5 0.0 copy-start.5
  120.5 0.6 copy-done.5
  121.1 46.7 %attend.2 = (bf16[512,2048]{1,0:T(8,128)(2,1)}, f32[16,256]{1,0:T(8,128)}) custom-call(s32[2]{0:T(128)} %copy-done.4, bf16[8,48,2048]{2,1,0:T(8,128)(2,1)} %copy-done, bf16[1,2048]{1,0:T(2,128)(2,1)} %reshape.35.refs_2_, f32[512,128]{1,0:T(8,128)} %copy-done.2, f32[512,128]{1,0:T(8,128)} %copy-done.3, bf16[2048,256]{1,0:T(8,128)(2,1)} %refs_5_.3, ...), custom_call_target="tpu_custom_call" | custom-call | flops 3221225472 | bytes 2097152 | tf_op jit(solution)/shard_map/attend/pallas_call | solution.py:179
  167.8 2.7 %collective-permute-start.2 = (f32[16,256]{1,0:T(8,128)}, f32[16,256]{1,0:T(8,128)S(1)}, u32[]{:S(2)}, u32[]{:S(2)}) collective-permute-start(f32[16,256]{1,0:T(8,128)} %get-tuple-element.31), channel_id=1, source_target_pairs={{0,3},{1,2},{2,1},{3,0},{4,7},{5,6},{6,5},{7,4},{8,11},{9,10},{10,... | collective-permute-start | bytes 49160 | tf_op jit(solution)/shard_map/ppermute | solution.py:256
  170.6 0.2 collective-permute-start.1
  170.8 0.2 collective-permute-start
  171.0 1.5 collective-permute-done.2
  172.6 0.8 collective-permute-done.1
  173.4 0.0 collective-permute-done
  173.4 1.4 fusion.1
  174.8 0.7 fusion.6
  178.1 0.0 all-to-all-done.2.refs_1_
  178.1 45.7 %attend.3 = (bf16[512,2048]{1,0:T(8,128)(2,1)}, f32[16,256]{1,0:T(8,128)}) custom-call(s32[2]{0:T(128)} %copy-done.4, bf16[8,32,2048]{2,1,0:T(8,128)(2,1)} %all-to-all-done.2.refs_1_, bf16[1,2048]{1,0:T(2,128)(2,1)} %reshape.35.refs_2_, f32[512,128]{1,0:T(8,128)} %copy-done.2, f32[512,128]{1,0:T(8,128)} %copy-done.3, ...), custom_call_target="tpu_custom_call", output_to_operand_aliasing={{0}: (10, {})} | custom-call | flops 3221225472 | bytes 2097152 | tf_op jit(solution)/shard_map/attend/pallas_call | solution.py:179
  (3 shorter events, 0.0 us)
Async XLA Ops:
  4.1 5.7 %copy-start.8 = (bf16[256]{0:T(256)(128)(2,1)S(1)}, bf16[256]{0:T(256)(128)(2,1)}, u32[]{:S(2)}) copy-start(bf16[256]{0:T(256)(128)(2,1)} %param.14) | copy-start | bytes 1540
  4.1 5.7 %copy-start.9 = (bf16[256]{0:T(256)(128)(2,1)S(1)}, bf16[256]{0:T(256)(128)(2,1)}, u32[]{:S(2)}) copy-start(bf16[256]{0:T(256)(128)(2,1)} %param.15) | copy-start | bytes 1540
  4.1 5.8 %copy-start.7 = (bf16[2048]{0:T(1024)(128)(2,1)S(1)}, bf16[2048]{0:T(1024)(128)(2,1)}, u32[]{:S(2)}) copy-start(bf16[2048]{0:T(1024)(128)(2,1)} %param.13) | copy-start | bytes 12292
  4.2 6.4 %copy-start.10 = (s32[8]{0:T(128)S(1)}, s32[8]{0:T(128)}, u32[]{:S(2)}) copy-start(s32[8]{0:T(128)} %param.19) | copy-start | bytes 100
  4.2 61.7 %all-to-all-start = ((bf16[8,80,2048]{2,1,0:T(8,128)(2,1)}), bf16[8,80,2048]{2,1,0:T(8,128)(2,1)S(1)}, u32[]{:S(2)}, u32[]{:S(2)}) async-start(bf16[8,80,2048]{2,1,0:T(8,128)(2,1)} %deal.1), calls=%async_computation | async-start | bytes 5242880 | tf_op jit(solution)/shard_map/all_to_all | solution.py:367
  11.9 106.6 %copy-start.4 = (s32[2]{0:T(128)}, s32[2]{0:T(128)S(1)}, u32[]{:S(2)}) copy-start(s32[2]{0:T(128)S(1)} %pad_add_fusion.meta.refs_0_) | copy-start | bytes 28
  13.7 104.8 %copy-start.2 = (f32[512,128]{1,0:T(8,128)}, f32[512,128]{1,0:T(8,128)S(1)}, u32[]{:S(2)}) copy-start(f32[512,128]{1,0:T(8,128)S(1)} %get-tuple-element.24.cos.refs_3_) | copy-start | bytes 786436
  13.7 104.7 %copy-start.3 = (f32[512,128]{1,0:T(8,128)}, f32[512,128]{1,0:T(8,128)S(1)}, u32[]{:S(2)}) copy-start(f32[512,128]{1,0:T(8,128)S(1)} %get-tuple-element.25.sin.refs_4_) | copy-start | bytes 786436
  65.8 1.5 copy-start.6
  70.3 40.9 %all-to-all-start.1 = ((bf16[8,48,2048]{2,1,0:T(8,128)(2,1)}), bf16[8,48,2048]{2,1,0:T(8,128)(2,1)S(1)}, u32[]{:S(2)}, u32[]{:S(2)}) async-start(bf16[8,48,2048]{2,1,0:T(8,128)(2,1)} %route.2), calls=%async_computation.1 | async-start | bytes 3145728 | tf_op jit(solution)/shard_map/all_to_all | solution.py:367
  77.7 40.8 %copy-start.1 = (bf16[2048,256]{1,0:T(8,128)(2,1)S(1)}, bf16[2048,256]{1,0:T(8,128)(2,1)}, u32[]{:S(2)}) copy-start(bf16[2048,256]{1,0:T(8,128)(2,1)} %refs_5_.3) | copy-start | bytes 3145732
  111.2 9.3 %copy-start = (bf16[8,48,2048]{2,1,0:T(8,128)(2,1)}, bf16[8,48,2048]{2,1,0:T(8,128)(2,1)S(1)}, u32[]{:S(2)}) copy-start(bf16[8,48,2048]{2,1,0:T(8,128)(2,1)S(1)} %all-to-all-done.1.arrived.refs_1_) | copy-start | bytes 4718596
  111.2 66.9 %all-to-all-start.2 = ((bf16[8,32,2048]{2,1,0:T(8,128)(2,1)}), bf16[8,32,2048]{2,1,0:T(8,128)(2,1)}, u32[]{:S(2)}, u32[]{:S(2)}) async-start(bf16[8,32,2048]{2,1,0:T(8,128)(2,1)} %route.3), calls=%async_computation.2 | async-start | bytes 2097152 | tf_op jit(solution)/shard_map/all_to_all | solution.py:367
  120.5 0.6 copy-start.5
  167.8 4.7 %collective-permute-start.2 = (f32[16,256]{1,0:T(8,128)}, f32[16,256]{1,0:T(8,128)S(1)}, u32[]{:S(2)}, u32[]{:S(2)}) collective-permute-start(f32[16,256]{1,0:T(8,128)} %get-tuple-element.31), channel_id=1, source_target_pairs={{0,3},{1,2},{2,1},{3,0},{4,7},{5,6},{6,5},{7,4},{8,11},{9,10},{10,... | collective-permute-start | bytes 49160 | tf_op jit(solution)/shard_map/ppermute | solution.py:256
  170.6 2.8 %collective-permute-start.1 = (f32[16,256]{1,0:T(8,128)}, f32[16,256]{1,0:T(8,128)S(1)}, u32[]{:S(2)}, u32[]{:S(2)}) collective-permute-start(f32[16,256]{1,0:T(8,128)} %get-tuple-element.31), channel_id=1, source_target_pairs={{0,2},{1,3},{2,0},{3,1},{4,6},{5,7},{6,4},{7,5},{8,10},{9,11},{10,... | collective-permute-start | bytes 49160 | tf_op jit(solution)/shard_map/ppermute | solution.py:256
  170.8 2.6 %collective-permute-start = (f32[16,256]{1,0:T(8,128)}, f32[16,256]{1,0:T(8,128)S(1)}, u32[]{:S(2)}, u32[]{:S(2)}) collective-permute-start(f32[16,256]{1,0:T(8,128)} %get-tuple-element.31), channel_id=1, source_target_pairs={{0,1},{1,0},{2,3},{3,2},{4,5},{5,4},{6,7},{7,6},{8,9},{9,8},{10,11... | collective-permute-start | bytes 49160 | tf_op jit(solution)/shard_map/ppermute | solution.py:256

commit v3 on v1

--- a/solution.py
+++ b/solution.py
@@ -155,7 +155,7 @@
     wide = group * HEAD
     fresh, cache_rows = news[0].shape[0], caches[0].shape[0]
     fresh_block = min(fresh, -(-(first + rows) // 256) * 256)
-    wide_block, block = math.gcd(1024, cache_rows), math.gcd(512, cache_rows)
+    wide_block, block = math.gcd(2048, cache_rows), math.gcd(512, cache_rows)
     column = lambda n, width: pl.BlockSpec((n, width), lambda g, m: (0, g))
     table = pl.BlockSpec((rows, HEAD), lambda g, m: (first // rows, 0))
     given = [] if out is None else [out]

time: 223 us -> 223 us (level)
  the two profiles are of different devices: /device:TPU:13 before, /device:TPU:21 now
where the time goes in v3:
time: 223 us; the launch traced here: 222 us
  Pallas kernels  104 us (47%)
  waiting for transfers between devices  82.7 us (37%)
  starting transfers between devices  23.5 us (11%)
  other arithmetic  4.5 us (2%)
  between operations  4.49 us (2%)
  local copies, waits for them, and re-layouts  2.77 us (1%)
    pallas_call x2, Pallas kernels, attend(): pl.pallas_call(functools.partial(attend_kernel, skip=height - size, first...  92.6 us
    all_to_all x3, waiting for transfers between devices, exchange(): return lax.all_to_all(x, 'seq', split_axis=0, concat_axis=0, tiled=True)  82.7 us
    all_to_all x3, starting transfers between devices, exchange(): return lax.all_to_all(x, 'seq', split_axis=0, concat_axis=0, tiled=True)  20.3 us
    pallas_call x2, Pallas kernels, route(): pl.pallas_call(functools.partial(route_kernel, span=span), in_specs=[SMEM...  5.86 us
  transfers between devices with their start and end apart: 6, of which 2 were waited for; matrix products, arithmetic and copies ran while one was open for 2% of the time, Pallas kernels for 44%

profile of v3, /device:TPU:21, one launch (start us, length us, event | category | flops | bytes accessed | tf_op | source)
XLA Modules:
  0.0 221.9 jit_solution(11222084490620496291)
XLA Ops:
  0.6 3.5 %deal.1 = bf16[8,80,2048]{2,1,0:T(8,128)(2,1)} custom-call(bf16[512,2048]{1,0:T(8,128)(2,1)} %q.1, bf16[512,256]{1,0:T(8,128)(2,1)} %k.1, bf16[512,256]{1,0:T(8,128)(2,1)} %v.1), custom_call_target="tpu_custom_call" | custom-call | tf_op jit(solution)/shard_map/deal/pallas_call | solution.py:295
  4.1 0.0 copy-start.9
  4.1 0.0 copy-start.10
  4.1 0.0 copy-start.8
  4.2 0.0 copy-start.11
  4.2 5.7 %all-to-all-start = ((bf16[8,80,2048]{2,1,0:T(8,128)(2,1)}), bf16[8,80,2048]{2,1,0:T(8,128)(2,1)S(1)}, u32[]{:S(2)}, u32[]{:S(2)}) async-start(bf16[8,80,2048]{2,1,0:T(8,128)(2,1)} %deal.1), calls=%async_computation | async-start | bytes 5242880 | tf_op jit(solution)/shard_map/all_to_all | solution.py:355
  9.9 0.0 copy-done.9
  9.9 0.0 copy-done.10
  9.9 0.0 copy-done.8
  9.9 0.6 reshape.35.refs_2_
  10.5 0.0 copy-done.11
  10.5 0.6 fusion.2
  11.2 0.7 pad_add_fusion.meta.refs_0_
  11.9 0.0 copy-start.4
  11.9 0.7 add_convert_fusion
  12.5 1.0 fusion
  13.5 0.2 pad_maximum_fusion
  13.7 0.0 copy-start.2
  13.8 0.0 copy-start.3
  13.8 52.1 %all-to-all-done.x = bf16[8,80,2048]{2,1,0:T(8,128)(2,1)S(1)} async-done(((bf16[8,80,2048]{2,1,0:T(8,128)(2,1)}), bf16[8,80,2048]{2,1,0:T(8,128)(2,1)S(1)}, u32[]{:S(2)}, u32[]{:S(2)}) %all-to-all-start) | async-done | bytes 2621472 | tf_op jit(solution)/shard_map/all_to_all | solution.py:355
  65.8 0.0 copy-start.6
  65.9 1.5 copy-done.6
  67.4 3.0 %route.3 = bf16[8,48,2048]{2,1,0:T(8,128)(2,1)} custom-call(s32[8]{0:T(128)} %deal.3, bf16[8,80,2048]{2,1,0:T(8,128)(2,1)} %copy-done.6), custom_call_target="tpu_custom_call" | custom-call | tf_op jit(solution)/shard_map/route/pallas_call | solution.py:321
  70.3 7.3 %all-to-all-start.2 = ((bf16[8,48,2048]{2,1,0:T(8,128)(2,1)}), bf16[8,48,2048]{2,1,0:T(8,128)(2,1)S(1)}, u32[]{:S(2)}, u32[]{:S(2)}) async-start(bf16[8,48,2048]{2,1,0:T(8,128)(2,1)} %route.3), calls=%async_computation.2 | async-start | bytes 3145728 | tf_op jit(solution)/shard_map/all_to_all | solution.py:355
  77.7 0.0 copy-start.1
  77.7 2.9 %route.2 = bf16[8,32,2048]{2,1,0:T(8,128)(2,1)} custom-call(s32[8]{0:T(128)} %deal.3, bf16[8,80,2048]{2,1,0:T(8,128)(2,1)} %copy-done.6), custom_call_target="tpu_custom_call" | custom-call | tf_op jit(solution)/shard_map/route/pallas_call | solution.py:321
  80.6 30.6 %all-to-all-done.2.arrived.refs_1_ = bf16[8,48,2048]{2,1,0:T(8,128)(2,1)S(1)} async-done(((bf16[8,48,2048]{2,1,0:T(8,128)(2,1)}), bf16[8,48,2048]{2,1,0:T(8,128)(2,1)S(1)}, u32[]{:S(2)}, u32[]{:S(2)}) %all-to-all-start.2) | async-done | bytes 1572896 | tf_op jit(solution)/shard_map/all_to_all | solution.py:355
  111.2 0.0 copy-start
  111.2 7.3 %all-to-all-start.1 = ((bf16[8,32,2048]{2,1,0:T(8,128)(2,1)}), bf16[8,32,2048]{2,1,0:T(8,128)(2,1)}, u32[]{:S(2)}, u32[]{:S(2)}) async-start(bf16[8,32,2048]{2,1,0:T(8,128)(2,1)} %route.2), calls=%async_computation.1 | async-start | bytes 2097152 | tf_op jit(solution)/shard_map/all_to_all | solution.py:355
  118.5 0.0 copy-done.4
  118.5 0.0 copy-done.2
  118.5 0.0 copy-done.3
  118.5 0.0 copy-done.1
  118.5 2.0 fresh.1
  120.5 0.0 copy-done
  120.5 0.0 copy-start.5
  120.5 0.6 copy-done.5
  121.1 46.7 %attend.2 = (bf16[512,2048]{1,0:T(8,128)(2,1)}, f32[16,256]{1,0:T(8,128)}) custom-call(s32[2]{0:T(128)} %copy-done.4, bf16[8,48,2048]{2,1,0:T(8,128)(2,1)} %copy-done, bf16[1,2048]{1,0:T(2,128)(2,1)} %reshape.35.refs_2_, f32[512,128]{1,0:T(8,128)} %copy-done.2, f32[512,128]{1,0:T(8,128)} %copy-done.3, bf16[2048,256]{1,0:T(8,128)(2,1)} %refs_5_.3, ...), custom_call_target="tpu_custom_call" | custom-call | flops 3221225472 | bytes 2097152 | tf_op jit(solution)/shard_map/attend/pallas_call | solution.py:179
  167.8 2.7 %collective-permute-start.2 = (f32[16,256]{1,0:T(8,128)}, f32[16,256]{1,0:T(8,128)S(1)}, u32[]{:S(2)}, u32[]{:S(2)}) collective-permute-start(f32[16,256]{1,0:T(8,128)} %get-tuple-element.30), channel_id=1, source_target_pairs={{0,3},{1,2},{2,1},{3,0},{4,7},{5,6},{6,5},{7,4},{8,11},{9,10},{10,... | collective-permute-start | bytes 49160 | tf_op jit(solution)/shard_map/ppermute | solution.py:256
  170.6 0.3 collective-permute-start.1
  170.8 0.2 collective-permute-start
  171.0 0.0 all-to-all-done.1.refs_1_
  171.0 0.0 copy-start.7
  171.0 45.8 %attend.3 = (bf16[512,2048]{1,0:T(8,128)(2,1)}, f32[16,256]{1,0:T(8,128)}) custom-call(s32[2]{0:T(128)} %copy-done.4, bf16[8,32,2048]{2,1,0:T(8,128)(2,1)} %all-to-all-done.1.refs_1_, bf16[1,2048]{1,0:T(2,128)(2,1)} %reshape.35.refs_2_, f32[512,128]{1,0:T(8,128)} %copy-done.2, f32[512,128]{1,0:T(8,128)} %copy-done.3, ...), custom_call_target="tpu_custom_call", output_to_operand_aliasing={{0}: (10, {})} | custom-call | flops 3221225472 | bytes 2097152 | tf_op jit(solution)/shard_map/attend/pallas_call | solution.py:179
  216.9 0.0 collective-permute-done.2
  216.9 0.0 collective-permute-done.1
  216.9 0.0 collective-permute-done
  216.9 0.0 copy-done.7
  216.9 0.6 fusion.1
  217.5 0.7 fusion.6
  (3 shorter events, 0.0 us)
Async XLA Ops:
  4.1 5.7 %copy-start.9 = (bf16[256]{0:T(256)(128)(2,1)S(1)}, bf16[256]{0:T(256)(128)(2,1)}, u32[]{:S(2)}) copy-start(bf16[256]{0:T(256)(128)(2,1)} %param.14) | copy-start | bytes 1540
  4.1 5.7 %copy-start.10 = (bf16[256]{0:T(256)(128)(2,1)S(1)}, bf16[256]{0:T(256)(128)(2,1)}, u32[]{:S(2)}) copy-start(bf16[256]{0:T(256)(128)(2,1)} %param.15) | copy-start | bytes 1540
  4.1 5.8 %copy-start.8 = (bf16[2048]{0:T(1024)(128)(2,1)S(1)}, bf16[2048]{0:T(1024)(128)(2,1)}, u32[]{:S(2)}) copy-start(bf16[2048]{0:T(1024)(128)(2,1)} %param.13) | copy-start | bytes 12292
  4.2 6.4 %copy-start.11 = (s32[8]{0:T(128)S(1)}, s32[8]{0:T(128)}, u32[]{:S(2)}) copy-start(s32[8]{0:T(128)} %param.19) | copy-start | bytes 100
  4.2 61.7 %all-to-all-start = ((bf16[8,80,2048]{2,1,0:T(8,128)(2,1)}), bf16[8,80,2048]{2,1,0:T(8,128)(2,1)S(1)}, u32[]{:S(2)}, u32[]{:S(2)}) async-start(bf16[8,80,2048]{2,1,0:T(8,128)(2,1)} %deal.1), calls=%async_computation | async-start | bytes 5242880 | tf_op jit(solution)/shard_map/all_to_all | solution.py:355
  11.9 106.6 %copy-start.4 = (s32[2]{0:T(128)}, s32[2]{0:T(128)S(1)}, u32[]{:S(2)}) copy-start(s32[2]{0:T(128)S(1)} %pad_add_fusion.meta.refs_0_) | copy-start | bytes 28
  13.7 104.7 %copy-start.2 = (f32[512,128]{1,0:T(8,128)}, f32[512,128]{1,0:T(8,128)S(1)}, u32[]{:S(2)}) copy-start(f32[512,128]{1,0:T(8,128)S(1)} %get-tuple-element.21.cos.refs_3_) | copy-start | bytes 786436
  13.8 104.7 %copy-start.3 = (f32[512,128]{1,0:T(8,128)}, f32[512,128]{1,0:T(8,128)S(1)}, u32[]{:S(2)}) copy-start(f32[512,128]{1,0:T(8,128)S(1)} %get-tuple-element.22.sin.refs_4_) | copy-start | bytes 786436
  65.8 1.5 copy-start.6
  70.3 40.9 %all-to-all-start.2 = ((bf16[8,48,2048]{2,1,0:T(8,128)(2,1)}), bf16[8,48,2048]{2,1,0:T(8,128)(2,1)S(1)}, u32[]{:S(2)}, u32[]{:S(2)}) async-start(bf16[8,48,2048]{2,1,0:T(8,128)(2,1)} %route.3), calls=%async_computation.2 | async-start | bytes 3145728 | tf_op jit(solution)/shard_map/all_to_all | solution.py:355
  77.7 40.8 %copy-start.1 = (bf16[2048,256]{1,0:T(8,128)(2,1)S(1)}, bf16[2048,256]{1,0:T(8,128)(2,1)}, u32[]{:S(2)}) copy-start(bf16[2048,256]{1,0:T(8,128)(2,1)} %refs_5_.3) | copy-start | bytes 3145732
  111.2 9.3 %copy-start = (bf16[8,48,2048]{2,1,0:T(8,128)(2,1)}, bf16[8,48,2048]{2,1,0:T(8,128)(2,1)S(1)}, u32[]{:S(2)}) copy-start(bf16[8,48,2048]{2,1,0:T(8,128)(2,1)S(1)} %all-to-all-done.2.arrived.refs_1_) | copy-start | bytes 4718596
  111.2 59.8 %all-to-all-start.1 = ((bf16[8,32,2048]{2,1,0:T(8,128)(2,1)}), bf16[8,32,2048]{2,1,0:T(8,128)(2,1)}, u32[]{:S(2)}, u32[]{:S(2)}) async-start(bf16[8,32,2048]{2,1,0:T(8,128)(2,1)} %route.2), calls=%async_computation.1 | async-start | bytes 2097152 | tf_op jit(solution)/shard_map/all_to_all | solution.py:355
  120.5 0.6 copy-start.5
  167.8 49.0 %collective-permute-start.2 = (f32[16,256]{1,0:T(8,128)}, f32[16,256]{1,0:T(8,128)S(1)}, u32[]{:S(2)}, u32[]{:S(2)}) collective-permute-start(f32[16,256]{1,0:T(8,128)} %get-tuple-element.30), channel_id=1, source_target_pairs={{0,3},{1,2},{2,1},{3,0},{4,7},{5,6},{6,5},{7,4},{8,11},{9,10},{10,... | collective-permute-start | bytes 49160 | tf_op jit(solution)/shard_map/ppermute | solution.py:256
  170.6 46.3 %collective-permute-start.1 = (f32[16,256]{1,0:T(8,128)}, f32[16,256]{1,0:T(8,128)S(1)}, u32[]{:S(2)}, u32[]{:S(2)}) collective-permute-start(f32[16,256]{1,0:T(8,128)} %get-tuple-element.30), channel_id=1, source_target_pairs={{0,2},{1,3},{2,0},{3,1},{4,6},{5,7},{6,4},{7,5},{8,10},{9,11},{10,... | collective-permute-start | bytes 49160 | tf_op jit(solution)/shard_map/ppermute | solution.py:256
  170.8 46.1 %collective-permute-start = (f32[16,256]{1,0:T(8,128)}, f32[16,256]{1,0:T(8,128)S(1)}, u32[]{:S(2)}, u32[]{:S(2)}) collective-permute-start(f32[16,256]{1,0:T(8,128)} %get-tuple-element.30), channel_id=1, source_target_pairs={{0,1},{1,0},{2,3},{3,2},{4,5},{5,4},{6,7},{7,6},{8,9},{9,8},{10,11... | collective-permute-start | bytes 49160 | tf_op jit(solution)/shard_map/ppermute | solution.py:256
  171.0 45.9 %copy-start.7 = (f32[16,256]{1,0:T(8,128)S(1)}, f32[16,256]{1,0:T(8,128)}, u32[]{:S(2)}) copy-start(f32[16,256]{1,0:T(8,128)} %get-tuple-element.30) | copy-start | bytes 49156
